TPU v7x, 256 devices: a whole 4x4x8 slice. The times are simulated.
256 devices in a mesh: worker: 32 (over z_lo, x, core), shard: 8 (over y, z_hi).
Axes of the slice: x: 4, y: 4, z: 8 (z_hi: 2, z_lo: 4; z = z_hi * 4 + z_lo), core: 2. Of those that a mesh axis runs over, the one named last changes fastest.
Arguments:
- local_w: bfloat16 [32, 2048, 4608], P('worker', 'shard'), may hold values from -36 to 36
- base_w: float32 [2048, 4608], P('shard'), may hold values from -6 to 6
- momentum: float32 [2048, 4608], P(('shard', 'worker')), may hold values from -3 to 3
Outputs:
- new_base: float32 [2048, 4608], P('shard')
- new_momentum: float32 [2048, 4608], P(('shard', 'worker'))
All inputs are finite; a program needn't handle non-finite values.
Results may differ from a plain program's by a relative error of at most 0.028.
Values may be sent and summed in bfloat16 or wider, within the bound.
A program may use at most 64 MiB of HBM per device.

v0:
```python
import math

import jax
import jax.numpy as jnp
from jax import lax
from jax.sharding import PartitionSpec as P

BLOCK = 128


epsilon = 1e-06
CODE_LIMIT = 448.0
CLIP_WIDTH = 2.0
NESTEROV_MU = 0.9
OUTER_RATE = 0.7


def signs_table():
    row_ids = lax.broadcasted_iota(jnp.int32, (BLOCK, BLOCK), 0)
    col_ids = lax.broadcasted_iota(jnp.int32, (BLOCK, BLOCK), 1)
    common_bits = jnp.bitwise_and(row_ids, col_ids)
    parity = jnp.zeros((BLOCK, BLOCK), jnp.int32)
    for bit_pos in range(BLOCK.bit_length() - 1):
        parity = parity + jnp.bitwise_and(jnp.right_shift(common_bits, bit_pos), 1)
    signs = 1 - 2 * jnp.bitwise_and(parity, 1)
    return signs.astype(jnp.float32) * (1.0 / math.sqrt(BLOCK))


def rotate(values, table):
    leading = values.shape[:-1]
    columns = values.shape[-1]
    blocks = values.reshape(leading + (columns // BLOCK, BLOCK))
    turned = jnp.matmul(blocks, table, precision=lax.Precision.HIGHEST)
    return turned.reshape(values.shape)


def encode_blocks(rotated):
    leading = rotated.shape[:-1]
    columns = rotated.shape[-1]
    blocks = rotated.reshape(leading + (columns // BLOCK, BLOCK))
    spread = jnp.sqrt(jnp.mean(blocks * blocks, axis=-1) + epsilon)
    block_scale = (CLIP_WIDTH * spread / CODE_LIMIT).astype(jnp.bfloat16)
    ratio = blocks / block_scale.astype(jnp.float32)[..., None]
    encoded = jnp.clip(ratio, -CODE_LIMIT, CODE_LIMIT).astype(jnp.bfloat16)
    return (encoded.reshape(rotated.shape), block_scale)


def decode_blocks(encoded, block_scale):
    leading = encoded.shape[:-1]
    columns = encoded.shape[-1]
    blocks = encoded.astype(jnp.float32).reshape(leading + (columns // BLOCK, BLOCK))
    blocks = blocks * block_scale.astype(jnp.float32)[..., None]
    return blocks.reshape(encoded.shape)


def shards(local_w, base_w, momentum):
    table = signs_table()
    workers = lax.axis_size("worker")
    pseudo_rows = base_w - local_w[0].astype(jnp.float32)
    encoded, block_scale = encode_blocks(rotate(pseudo_rows, table))
    got_codes, got_scale = (
        lax.all_to_all(encoded[None], "worker", split_axis=1, concat_axis=0, tiled=True),
        lax.all_to_all(block_scale[None], "worker", split_axis=1, concat_axis=0, tiled=True),
    )
    decoded = decode_blocks(got_codes, got_scale)
    summed = jnp.sum(rotate(decoded, table), axis=0)
    pseudo = summed * (1.0 / workers)
    new_momentum = NESTEROV_MU * momentum + pseudo
    outer_step = pseudo + NESTEROV_MU * new_momentum
    step_codes, step_scale = encode_blocks(rotate(outer_step, table))
    all_codes, all_scale = (
        lax.all_gather(step_codes, "worker", axis=0, tiled=True),
        lax.all_gather(step_scale, "worker", axis=0, tiled=True),
    )
    new_base = base_w - OUTER_RATE * rotate(decode_blocks(all_codes, all_scale), table)
    return (new_base, new_momentum)


def solution(mesh):
    in_specs = (P("worker", "shard", None), P("shard", None), P(("shard", "worker"), None))
    out_specs = (P("shard", None), P(("shard", "worker"), None))
    return jax.shard_map(shards, mesh=mesh, in_specs=in_specs, out_specs=out_specs, check_vma=False)
```

profile of v0, /device:TPU:1, one launch (start us, length us, event | category | flops | bytes accessed | tf_op | source)
XLA Modules:
  0.0 240.4 jit_solution(12244365617412863985)
XLA Ops:
  7.2 2.8 %copy.75 = bf16[1,256,4608]{1,2,0:T(8,128)(2,1)S(1)} copy(bf16[1,256,4608]{2,1,0:T(8,128)(2,1)} %param.3) | data formatting | bytes 4718592 | tf_op args[0]
  10.0 6.0 %copy.76 = f32[256,4608]{0,1:T(8,128)} copy(f32[256,4608]{1,0:T(8,128)} %param.4) | data formatting | bytes 9437184 | tf_op args[1]
  16.1 2.8 %convert_subtract_fusion = f32[256,4608]{0,1:T(8,128)S(1)} fusion(f32[256,4608]{0,1:T(8,128)} %copy.76, bf16[1,256,4608]{1,2,0:T(8,128)(2,1)S(1)} %copy.75), kind=kLoop, calls=%fused_computation.3 | loop fusion | flops 2359296 | bytes 11796480 | tf_op jit(solution)/shard_map/sub | solution.py:59
  18.8 6.1 %multiply_reduce_fusion = (f32[256,36]{0,1:T(8,128)S(1)}, f32[256,36,128]{0,2,1:T(8,128)}) fusion(f32[256,36,128]{0,2,1:T(8,128)S(1)} %bitcast.54), kind=kOutput, calls=%fused_computation.7 | convolution fusion | flops 1814715392 | bytes 9474048 | tf_op jit(solution)/shard_map/dot_general | solution.py:33
  25.0 0.1 copy.80
  25.1 0.6 broadcast.116
  25.7 1.1 reduce.2
  26.8 0.7 reshape.104
  27.6 10.0 %all-to-all-start.1 = ((bf16[32,2,144]{2,1,0:T(2,128)(2,1)}), bf16[32,2,144]{2,1,0:T(2,128)(2,1)S(1)}, u32[]{:S(2)}, u32[]{:S(2)}) async-start(bf16[32,2,144]{2,1,0:T(2,128)(2,1)} %reshape.104), calls=%async_computation.1 | async-start | bytes 65536 | tf_op jit(solution)/shard_map/all_to_all | solution.py:63
  37.6 3.1 %clamp_convert_fusion = bf16[256,36,128]{0,2,1:T(8,128)(2,1)S(1)} fusion(f32[256,36,128]{0,2,1:T(8,128)} %get-tuple-element.9, f32[256,36]{0,1:T(8,128)S(1)} %get-tuple-element.7), kind=kLoop, calls=%fused_computation.6 | loop fusion | flops 3538944 | bytes 7114752 | tf_op jit(solution)/shard_map/convert_element_type | solution.py:44
  40.7 8.5 %copy.78 = bf16[1,256,4608]{2,0,1:T(2,128)(2,1)} copy(bf16[1,256,4608]{1,2,0:T(8,128)(2,1)S(1)} %bitcast.55) | data formatting | bytes 4718592 | tf_op jit(solution)/shard_map/broadcast_in_dim;reshape | solution.py:62
  49.2 14.8 %reduce.1 = bf16[256,4608]{1,0:T(8,128)(2,1)S(1)} reduce(bf16[256,1,4608]{2,1,0:T(2,128)(2,1)} %bitcast.51, bf16[]{:T(256)} %broadcast.116), dimensions={1}, to_apply=%bitcast.39.reduce_sub_computation | reduce | bytes 4718594
  64.1 2.3 reshape.102
  66.4 7.7 %all-to-all-start = ((bf16[32,2,18432]{2,1,0:T(2,128)(2,1)}), bf16[32,2,18432]{2,1,0:T(2,128)(2,1)S(1)}, u32[]{:S(2)}, u32[]{:S(2)}) async-start(bf16[32,2,18432]{2,1,0:T(2,128)(2,1)} %reshape.102), calls=%async_computation | async-start | bytes 4718592 | tf_op jit(solution)/shard_map/all_to_all | solution.py:62
  74.1 0.2 all-gather.2.cloned.1.call-start
  74.4 0.1 reshape.105
  74.5 0.3 copy.82
  74.8 53.1 %all-to-all-done = bf16[32,2,18432]{2,1,0:T(2,128)(2,1)S(1)} async-done(((bf16[32,2,18432]{2,1,0:T(2,128)(2,1)}), bf16[32,2,18432]{2,1,0:T(2,128)(2,1)S(1)}, u32[]{:S(2)}, u32[]{:S(2)}) %all-to-all-start) | async-done | bytes 2359328 | tf_op jit(solution)/shard_map/all_to_all | solution.py:62
  127.9 6.9 %reshape.103 = bf16[256,1,4608]{2,1,0:T(2,128)(2,1)} reshape(bf16[32,2,18432]{2,1,0:T(2,128)(2,1)S(1)} %all-to-all-done) | data formatting | bytes 4718592
  134.8 4.2 %convert_multiply_fusion = f32[32,8,36,128]{3,1,2,0:T(8,128)S(1)} fusion(bf16[1,256,4608]{2,0,1:T(2,128)(2,1)} %bitcast.50, f32[32,8,36]{1,2,0:T(8,128)S(1)} %copy.82), kind=kLoop, calls=%fused_computation.2 | loop fusion | flops 2359296 | bytes 7114752 | tf_op jit(solution)/shard_map/mul | solution.py:52
  139.1 4.6 %fusion.7 = f32[8,36,128]{2,1,0:T(8,128)S(1)} fusion(f32[32,8,36,128]{3,1,2,0:T(8,128)S(1)} %convert_multiply_fusion), kind=kOutput, calls=%fused_computation.10 | convolution fusion | flops 1813508096 | bytes 4866048 | tf_op jit(solution)/shard_map/dot_general | solution.py:33
  143.7 0.7 fusion.12
  144.4 0.4 multiply_reduce_fusion.1
  144.8 0.1 fusion.13
  144.9 0.6 copy.113
  145.6 42.2 %all_gather.7 = bf16[256,36]{1,0:T(8,128)(2,1)S(1)} all-gather(bf16[8,36]{1,0:T(8,128)(2,1)S(1)} %get-tuple-element.3), channel_id=1, replica_groups=mesh['worker'=32,'shard'=8] {'worker'}, dimensions={0}, use_global_device_ids=true | all-gather | bytes 19008 | tf_op jit(solution)/shard_map/all_gather | solution.py:73
  187.8 0.1 copy.88
  187.9 19.3 %all-gather.2.cloned.1.call-done = bf16[256,4608]{1,0:T(8,128)(2,1)} async-done(((bf16[8,4608]{1,0:T(8,128)(2,1)}), bf16[256,4608]{1,0:T(8,128)(2,1)}) %all-gather.2.cloned.1.call-update) | async-done | bytes 2359312 | tf_op jit(solution)/shard_map/all_gather | solution.py:72
  207.2 4.5 %copy.87 = f32[256,4608]{0,1:T(8,128)} copy(bf16[256,4608]{1,0:T(8,128)(2,1)} %all-gather.2.cloned.1.call-done) | data formatting | bytes 7077888 | tf_op jit(solution)/shard_map/reshape | solution.py:51
  211.7 9.2 %broadcast_multiply_fusion = f32[256,36,128]{0,2,1:T(8,128)} fusion(f32[256,36,128]{0,2,1:T(8,128)} %bitcast.52, f32[256,36]{0,1:T(8,128)S(1)} %convert_element_type.90), kind=kOutput, calls=%fused_computation.8 | convolution fusion | flops 1814724608 | bytes 9474048 | tf_op jit(solution)/shard_map/dot_general | solution.py:33
  221.0 6.0 %copy.90 = f32[256,4608]{1,0:T(8,128)} copy(f32[256,4608]{0,1:T(8,128)} %bitcast.53) | data formatting | bytes 9437184 | tf_op jit(solution)/shard_map/mul | solution.py:75
  227.0 6.5 %sub.17 = f32[256,4608]{1,0:T(8,128)} subtract(f32[256,4608]{1,0:T(8,128)} %param.4, f32[256,4608]{1,0:T(8,128)} %copy.90) | non-fusion elementwise | flops 1179648 | bytes 14155776 | tf_op jit(solution)/shard_map/sub | solution.py:75
  (9 shorter events, 0.1 us)
Async XLA Ops:
  27.6 38.8 %all-to-all-start.1 = ((bf16[32,2,144]{2,1,0:T(2,128)(2,1)}), bf16[32,2,144]{2,1,0:T(2,128)(2,1)S(1)}, u32[]{:S(2)}, u32[]{:S(2)}) async-start(bf16[32,2,144]{2,1,0:T(2,128)(2,1)} %reshape.104), calls=%async_computation.1 | async-start | bytes 65536 | tf_op jit(solution)/shard_map/all_to_all | solution.py:63
  66.4 61.5 %all-to-all-start = ((bf16[32,2,18432]{2,1,0:T(2,128)(2,1)}), bf16[32,2,18432]{2,1,0:T(2,128)(2,1)S(1)}, u32[]{:S(2)}, u32[]{:S(2)}) async-start(bf16[32,2,18432]{2,1,0:T(2,128)(2,1)} %reshape.102), calls=%async_computation | async-start | bytes 4718592 | tf_op jit(solution)/shard_map/all_to_all | solution.py:62
  74.1 133.1 %all-gather.2.cloned.1.call-start = ((), (), s32[]{:S(2)}) async-start(), calls=%async_computation.2 | async-start | bytes 2433024 | tf_op jit(solution)/shard_map/all_gather | solution.py:72
  139.1 4.6 %copy-start = (f32[8,4608]{1,0:T(8,128)S(1)}, f32[8,4608]{1,0:T(8,128)}, u32[]{:S(2)}) copy-start(f32[8,4608]{1,0:T(8,128)} %param.5) | copy-start | bytes 442372
Sparse Core Ops, SparseCore 0:
  145.7 61.4 all-gather.1
where the time goes:
time: 241 us; the launch traced here: 240 us
  waiting for transfers between devices  72.4 us (30%)
  blocking collectives  42.2 us (18%)
  local copies, waits for them, and re-layouts  39.8 us (17%)
  other arithmetic  33.5 us (14%)
  matrix products  20.3 us (8%)
  starting transfers between devices  18 us (7%)
  between operations  14.2 us (6%)
    all_to_all x1, waiting for transfers between devices, shards(): lax.all_to_all(encoded[None], 'worker', split_axis=1, concat_axis=0, tile...  53.1 us
    all_gather x1, blocking collectives, shards(): lax.all_gather(step_scale, 'worker', axis=0, tiled=True)  42.2 us
    dot_general x4, matrix products, rotate(): turned = jnp.matmul(blocks, table, precision=lax.Precision.HIGHEST)  20.3 us
    unnamed x10, local copies, waits for them, and re-layouts  20.2 us
    all_gather x1, waiting for transfers between devices, shards(): lax.all_gather(step_codes, 'worker', axis=0, tiled=True)  19.3 us
    unnamed x4, other arithmetic  16 us
    all_to_all x1, starting transfers between devices, shards(): lax.all_to_all(block_scale[None], 'worker', split_axis=1, concat_axis=0,...  10 us
    another operation x1, local copies, waits for them, and re-layouts, shards(): encoded[None]  8.48 us
  transfers between devices with their start and end apart: 3, of which 2 were waited for; matrix products, arithmetic and copies ran while one was open for 12% of the time, Pallas kernels for 0%

commit v1 on v0

v1 whole, which is shorter than its diff:
```python
import functools
import math

import jax
import jax.numpy as jnp
from jax import lax
from jax.experimental import pallas as pl
from jax.experimental.pallas import tpu as pltpu
from jax.sharding import PartitionSpec as P

MESH = pl.DeviceIdType.MESH
F32 = jnp.float32
BF16 = jnp.bfloat16

BLOCK = 128
WORKERS = 32
EPSILON = 1e-06
CODE_LIMIT = 448.0
CLIP_WIDTH = 2.0
NESTEROV_MU = 0.9
OUTER_RATE = 0.7
ROOT = math.sqrt(BLOCK)

ZS, XS, CORES = 4, 4, 2
ROWS = 8
GROUP = 16
SHIFT = (0, -2, 1, 1)


def signs(size):
    row = lax.broadcasted_iota(jnp.int32, (size, size), 0)
    col = lax.broadcasted_iota(jnp.int32, (size, size), 1)
    common = jnp.bitwise_and(jnp.bitwise_and(row, col), BLOCK - 1)
    for shift in (4, 2, 1):
        common = jnp.bitwise_xor(common, jnp.right_shift(common, shift))
    sign = (1 - 2 * jnp.bitwise_and(common, 1)).astype(F32)
    same = jnp.right_shift(row, 7) == jnp.right_shift(col, 7)
    return jnp.where(same, sign, 0.0).astype(BF16), jnp.where(same, 1.0, 0.0).astype(BF16)


def limit_of(square_sum):
    mean = square_sum * (1.0 / BLOCK) + EPSILON
    scale = (mean * lax.rsqrt(mean) * (CLIP_WIDTH / CODE_LIMIT)).astype(BF16)
    return scale.astype(F32)


def rotate_exactly(values, table):
    high = values.astype(BF16)
    low = (values - high.astype(F32)).astype(BF16)
    return jnp.dot(high, table, preferred_element_type=F32) + jnp.dot(low, table, preferred_element_type=F32)


def kernel(
    halves,
    local_hbm, base_hbm, mom_hbm,
    out_hbm, out_mom_hbm,
    local_v, base_v, mom_v, out_v, table2, ones2,
    enc, sib, ring_a, ring_l, ring_r, zsend, zrecv, acc, gath,
    in_sem, mom_sem, out_sem, mom_out_sem,
    sib_s, sib_r, a_s, a_r, b_s, b_r, c_s, c_r, z_s, z_r,
    gz_s, gz_r, gf_s, gf_r, gh_s, gh_r, gs_s, gs_r,
):
    me = lax.axis_index("worker")
    z, x, core = me // 8, (me // 2) % 4, me % 2
    inner = lax.rem(z, 3) != 0
    zz = jnp.minimum(z, 3 - z)
    high = z // 2
    tiles = halves * 2

    def order(s):
        first = (3 - s) + zz * SHIFT[s]
        return first + high * (3 - 2 * first)

    def at(z_, x_, core_):
        return {"worker": (z_ * XS + x_) * CORES + core_}

    xr, xl, xo = (x + 1) % XS, (x + XS - 1) % XS, (x + 2) % XS
    right, left, pair = at(z, xr, core), at(z, xl, core), at(z, x, 1 - core)
    toward, away = 1 - 2 * high, 2 * high - 1

    zds = [order(s) for s in range(ZS)]
    rows_of = [pl.ds(pl.multiple_of(zd * 64, 64), 64) for zd in zds]

    def copy(src, dst, send, recv, device):
        return pltpu.make_async_remote_copy(
            src_ref=src, dst_ref=dst, send_sem=send, recv_sem=recv, device_id=device, device_id_type=MESH
        )

    loads = []
    for s in range(ZS):
        loads.append((
            pltpu.make_async_copy(base_hbm.at[rows_of[s]], base_v.at[rows_of[s]], in_sem.at[s, 0]),
            pltpu.make_async_copy(local_hbm.at[0, rows_of[s]], local_v.at[rows_of[s]], in_sem.at[s, 1]),
        ))
        for one in loads[s]:
            one.start()
    mom_load = pltpu.make_async_copy(mom_hbm, mom_v, mom_sem)
    mom_load.start()

    barrier = pltpu.get_barrier_semaphore()
    for device in (right, left, pair, at(z + toward, x, core)):
        pl.semaphore_signal(barrier, inc=1, device_id=device, device_id_type=MESH)

    @pl.when(inner)
    def _():
        pl.semaphore_signal(barrier, inc=1, device_id=at(z + away, x, core), device_id_type=MESH)

    table, ones = signs(2 * BLOCK)
    table2[...] = table
    ones2[...] = ones

    def encode(s):
        for one in loads[s]:
            one.wait()
        zd = zds[s]

        def half_loop(half, carry):
            for k in range(halves):
                cols = pl.ds(pl.multiple_of((half * halves + k) * 256, 256), 256)
                diff = base_v[rows_of[s], cols] - local_v[rows_of[s], cols].astype(F32)
                turned = jnp.dot(diff.astype(BF16), table2[...], preferred_element_type=F32)
                square = jnp.dot((diff * diff).astype(BF16), ones2[...], preferred_element_type=F32)
                limit = limit_of(square) * (CODE_LIMIT * ROOT)
                value = jnp.minimum(jnp.maximum(turned, -limit), limit)
                for xd in range(XS):
                    for c in range(CORES):
                        r = xd * GROUP + c * ROWS
                        both = jnp.concatenate(
                            [value[r : r + ROWS, :BLOCK], value[r : r + ROWS, BLOCK:]], axis=0
                        )
                        enc[c, zd, xd, half, :, pl.ds(k * BLOCK, BLOCK)] = both.astype(BF16)
            return carry

        lax.fori_loop(0, 2, half_loop, 0)

    def send_pair(s):
        c = copy(enc.at[1 - core, zds[s]], sib.at[s], sib_s.at[s], sib_r.at[s], pair)
        c.start()
        return [c]

    def add_pair(s):
        zd = zds[s]
        copy(sib.at[s], sib.at[s], sib_s.at[s], sib_r.at[s], pair).wait_recv()
        for xd in range(XS):
            for half in range(2):
                enc[core, zd, xd, half] = (
                    enc[core, zd, xd, half].astype(F32) + sib[s, xd, half].astype(F32)
                ).astype(BF16)
        sent = [
            copy(enc.at[core, zd, xo, 0], ring_a.at[s, 0], a_s.at[s, 0], a_r.at[s, 0], right),
            copy(enc.at[core, zd, xo, 1], ring_a.at[s, 1], a_s.at[s, 1], a_r.at[s, 1], left),
            copy(enc.at[core, zd, xr, 1], ring_l.at[s, 1], b_s.at[s, 0], b_r.at[s, 0], right),
            copy(enc.at[core, zd, xl, 0], ring_r.at[s, 0], b_s.at[s, 1], b_r.at[s, 1], left),
        ]
        for one in sent:
            one.start()
        return sent

    def add_far(s):
        zd = zds[s]
        sent = []
        for half, to, device, land in ((0, xr, right, ring_l), (1, xl, left, ring_r)):
            copy(ring_a.at[s, half], ring_a.at[s, half], a_s.at[s, half], a_r.at[s, half], device).wait_recv()
            enc[core, zd, to, half] = (
                enc[core, zd, to, half].astype(F32) + ring_a[s, half].astype(F32)
            ).astype(BF16)
            sent.append(copy(enc.at[core, zd, to, half], land.at[s, half], c_s.at[s, half], c_r.at[s, half], device))
            sent[-1].start()
        return sent

    def add_ring(s):
        zd = zds[s]
        copy(ring_l.at[s, 1], ring_l.at[s, 1], b_s.at[s, 0], b_r.at[s, 0], right).wait_recv()
        copy(ring_r.at[s, 0], ring_r.at[s, 0], b_s.at[s, 1], b_r.at[s, 1], left).wait_recv()
        copy(ring_l.at[s, 0], ring_l.at[s, 0], c_s.at[s, 0], c_r.at[s, 0], right).wait_recv()
        copy(ring_r.at[s, 1], ring_r.at[s, 1], c_s.at[s, 1], c_r.at[s, 1], left).wait_recv()

        def total(half):
            return (
                enc[core, zd, x, half].astype(F32) + ring_l[s, half].astype(F32) + ring_r[s, half].astype(F32)
            )

        def arrived(which, way):
            copy(zrecv.at[which, way], zrecv.at[which, way], z_s.at[0], z_r.at[which, way], pair).wait_recv()

        if s < ZS - 1:
            way = (zd < z).astype(jnp.int32)

            @pl.when(inner)
            def _():
                arrived(zd, way)
                for half in range(2):
                    zsend[s, half] = (total(half) + zrecv[zd, way, half].astype(F32)).astype(BF16)

            @pl.when(jnp.logical_not(inner))
            def _():
                for half in range(2):
                    zsend[s, half] = total(half).astype(BF16)

            c = copy(zsend.at[s], zrecv.at[zd, way], z_s.at[s], z_r.at[zd, way], at(z + 1 - 2 * way, x, core))
            c.start()
            return [c]

        for half in range(2):
            acc[half] = total(half)
        for way, there in ((0, z > 0), (1, z < ZS - 1)):

            @pl.when(there)
            def _():
                arrived(z, way)
                for half in range(2):
                    acc[half] += zrecv[z, way, half].astype(F32)

        return []

    sends = []
    encode(0)
    pl.semaphore_wait(barrier, 4 + inner.astype(jnp.int32))
    sends += send_pair(0)
    encode(1)
    sends += send_pair(1)
    sends += add_pair(0)
    encode(2)
    sends += send_pair(2)
    sends += add_far(0)
    sends += add_pair(1)
    encode(3)
    sends += send_pair(3)
    sends += add_far(1)
    sends += add_pair(2)
    sends += add_ring(0)
    sends += add_far(2)
    sends += add_pair(3)
    sends += add_ring(1)
    sends += add_far(3)
    sends += add_ring(2)
    mom_load.wait()
    sends += add_ring(3)

    table1 = table2[:BLOCK, :BLOCK]

    def stacked(read):
        return jnp.concatenate([read(k) for k in range(tiles)], axis=0)

    def cut(array, k):
        return array[k * GROUP : (k + 1) * GROUP]

    total = stacked(lambda k: acc[k // halves, :, (k % halves) * BLOCK : (k % halves + 1) * BLOCK])
    momentum = stacked(
        lambda k: jnp.concatenate(
            [mom_v[:, 256 * k : 256 * k + BLOCK], mom_v[:, 256 * k + BLOCK : 256 * (k + 1)]], axis=0
        )
    )
    pseudo = rotate_exactly(total, table1) * (1.0 / (BLOCK * WORKERS))
    new_momentum = NESTEROV_MU * momentum + pseudo
    for k in range(tiles):
        one = cut(new_momentum, k)
        mom_v[:, 256 * k : 256 * k + BLOCK] = one[:ROWS]
        mom_v[:, 256 * k + BLOCK : 256 * (k + 1)] = one[ROWS:]
    mom_store = pltpu.make_async_copy(mom_v, out_mom_hbm, mom_out_sem)
    mom_store.start()
    outer_step = pseudo + NESTEROV_MU * new_momentum
    square = jnp.sum(outer_step * outer_step, axis=-1, keepdims=True)
    limit = limit_of(square) * CODE_LIMIT
    turned = rotate_exactly(outer_step, table1) * (1.0 / ROOT)
    value = jnp.minimum(jnp.maximum(turned, -limit), limit).astype(BF16)
    for k in range(tiles):
        gath[core, z, x, k // halves, :, (k % halves) * BLOCK : (k % halves + 1) * BLOCK] = cut(value, k)

    zos = [zds[ZS - 1 - s] for s in range(ZS)]

    def own_z():
        c = copy(gath.at[core, z, x], gath.at[core, z, x], gz_s.at[0], gz_r.at[z], at(z + toward, x, core))
        c.start()

        @pl.when(inner)
        def _():
            copy(gath.at[core, z, x], gath.at[core, z, x], gz_s.at[4], gz_r.at[z], at(z + away, x, core)).start()

        return [c]

    def next_z(s):
        zo = zos[s]
        spot = gath.at[core, zo, x]
        copy(spot, spot, gz_s.at[s], gz_r.at[zo], pair).wait_recv()

        @pl.when(inner)
        def _():
            to = z + 2 * (zo < z).astype(jnp.int32) - 1
            copy(spot, spot, gz_s.at[s], gz_r.at[zo], at(to, x, core)).start()

    def to_pair(s, i, x_):
        spot = gath.at[core, zos[s], x_]
        c = copy(spot, spot, gs_s.at[s, i], gs_r.at[s, i], pair)
        c.start()
        return [c]

    def full(s):
        spot = gath.at[core, zos[s], x]
        sent = [
            copy(spot, spot, gf_s.at[s, 0], gf_r.at[s, 0], right),
            copy(spot, spot, gf_s.at[s, 1], gf_r.at[s, 1], left),
        ]
        for one in sent:
            one.start()
        return sent + to_pair(s, 0, x)

    def onward(s):
        sent = []
        for half, x_, device in ((0, xl, right), (1, xr, left)):
            spot = gath.at[core, zos[s], x_]
            copy(spot, spot, gf_s.at[s, half], gf_r.at[s, half], device).wait_recv()
            sent.append(copy(spot.at[half], spot.at[half], gh_s.at[s, half], gh_r.at[s, half], device))
            sent[-1].start()
            sent += to_pair(s, 1 + half, x_)
        return sent

    def far(s):
        spot = gath.at[core, zos[s], xo]
        for half in range(2):
            copy(spot.at[half], spot.at[half], gh_s.at[s, half], gh_r.at[s, half], pair).wait_recv()
        return to_pair(s, 3, xo)

    def decode(s, c, x_):
        zo = zos[s]
        rows = pl.ds(pl.multiple_of((zo * XS + x_) * GROUP + c * ROWS, ROWS), ROWS)
        codes = stacked(lambda k: gath[c, zo, x_, k // halves, :, (k % halves) * BLOCK : (k % halves + 1) * BLOCK])
        back = jnp.dot(codes, table1, preferred_element_type=F32) * (OUTER_RATE / ROOT)
        for k in range(tiles):
            one = cut(back, k)
            for b in range(2):
                cols = slice(256 * k + b * BLOCK, 256 * k + (b + 1) * BLOCK)
                out_v[rows, cols] = base_v[rows, cols] - one[b * ROWS : (b + 1) * ROWS]

    def finish(s):
        zo = zos[s]

        def mine(x_, carry):
            decode(s, core, x_)
            return carry

        lax.fori_loop(0, XS, mine, 0)
        for i, x_ in enumerate((x, xl, xr, xo)):
            spot = gath.at[1 - core, zo, x_]
            copy(spot, spot, gs_s.at[s, i], gs_r.at[s, i], pair).wait_recv()

        def others(x_, carry):
            decode(s, 1 - core, x_)
            return carry

        lax.fori_loop(0, XS, others, 0)
        rows = rows_of[ZS - 1 - s]
        store = pltpu.make_async_copy(out_v.at[rows], out_hbm.at[rows], out_sem.at[s])
        store.start()
        return store

    stores = []
    sends += own_z()
    sends += full(0)
    next_z(1)
    sends += full(1)
    sends += onward(0)
    next_z(2)
    sends += full(2)
    sends += onward(1)
    sends += far(0)
    stores.append(finish(0))
    next_z(3)
    sends += full(3)
    sends += onward(2)
    sends += far(1)
    stores.append(finish(1))
    sends += onward(3)
    sends += far(2)
    stores.append(finish(2))
    sends += far(3)
    stores.append(finish(3))

    for one in sends:
        one.wait_send()

    @pl.when(inner)
    def _():
        for i in range(1, 5):
            spot = gath.at[core, z, x]
            copy(spot, spot, gz_s.at[i], gz_r.at[z], pair).wait_send()

    for store in stores:
        store.wait()
    mom_store.wait()


def step(local_w, base_w, momentum):
    rows, columns = base_w.shape
    halves = columns // 512
    width = halves * BLOCK
    dma = pltpu.SemaphoreType.DMA
    chunk = (2, GROUP, width)
    return pl.pallas_call(
        functools.partial(kernel, halves),
        out_shape=(
            jax.ShapeDtypeStruct(base_w.shape, F32),
            jax.ShapeDtypeStruct(momentum.shape, F32),
        ),
        in_specs=[pl.BlockSpec(memory_space=pl.ANY)] * 3,
        out_specs=[pl.BlockSpec(memory_space=pl.ANY)] * 2,
        scratch_shapes=[
            pltpu.VMEM((rows, columns), BF16),
            pltpu.VMEM((rows, columns), F32),
            pltpu.VMEM((ROWS, columns), F32),
            pltpu.VMEM((rows, columns), F32),
            pltpu.VMEM((2 * BLOCK, 2 * BLOCK), BF16),
            pltpu.VMEM((2 * BLOCK, 2 * BLOCK), BF16),
            pltpu.VMEM((CORES, ZS, XS) + chunk, BF16),
            pltpu.VMEM((ZS, XS) + chunk, BF16),
            pltpu.VMEM((ZS,) + chunk, BF16),
            pltpu.VMEM((ZS,) + chunk, BF16),
            pltpu.VMEM((ZS,) + chunk, BF16),
            pltpu.VMEM((ZS - 1,) + chunk, BF16),
            pltpu.VMEM((ZS, 2) + chunk, BF16),
            pltpu.VMEM(chunk, F32),
            pltpu.VMEM((CORES, ZS, XS) + chunk, BF16),
            dma((ZS, 2)), dma, dma((ZS,)), dma,
            dma((ZS,)), dma((ZS,)),
            dma((ZS, 2)), dma((ZS, 2)),
            dma((ZS, 2)), dma((ZS, 2)),
            dma((ZS, 2)), dma((ZS, 2)),
            dma((ZS - 1,)), dma((ZS, 2)),
            dma((5,)), dma((ZS,)),
            dma((ZS, 2)), dma((ZS, 2)),
            dma((ZS, 2)), dma((ZS, 2)),
            dma((ZS, 4)), dma((ZS, 4)),
        ],
        compiler_params=pltpu.CompilerParams(
            collective_id=0, has_side_effects=True, vmem_limit_bytes=60 * 1024 * 1024
        ),
    )(local_w, base_w, momentum)


def solution(mesh):
    in_specs = (P("worker", "shard", None), P("shard", None), P(("shard", "worker"), None))
    out_specs = (P("shard", None), P(("shard", "worker"), None))
    return jax.shard_map(step, mesh=mesh, in_specs=in_specs, out_specs=out_specs, check_vma=False)
```

time: 241 us -> 60.2 us (0.25)
  waiting for transfers between devices: 72.4 us -> 0 us
  Pallas kernels: 0 us -> 54 us
  blocking collectives: 42.2 us -> 0 us
  local copies, waits for them, and re-layouts: 39.8 us -> 5.54 us
  other arithmetic: 33.5 us -> 0 us
  matrix products: 20.3 us -> 0 us
  starting transfers between devices: 18 us -> 0 us
  between operations: 14.2 us -> 0.65 us
    pallas_call x0 -> x1, Pallas kernels: none -> 54 us  [step(): pl.pallas_call(functools.partial(kernel, halves), out_shape=(jax.ShapeDty...]
    all_to_all x2 -> x0, waiting for transfers between devices: 53.1 us -> none  [the longest x1 53.1 us: shards(): lax.all_to_all(encoded[None], 'worker', split_axis=1, concat_axis=0, tile...]
    all_gather x1 -> x0, blocking collectives: 42.2 us -> none  [shards(): lax.all_gather(step_scale, 'worker', axis=0, tiled=True)]
    dot_general x4 -> x0, matrix products: 20.3 us -> none  [rotate(): turned = jnp.matmul(blocks, table, precision=lax.Precision.HIGHEST)]
    all_gather x1 -> x0, waiting for transfers between devices: 19.3 us -> none  [shards(): lax.all_gather(step_codes, 'worker', axis=0, tiled=True)]
    all_to_all x2 -> x0, starting transfers between devices: 17.8 us -> none  [the longest x1 10 us: shards(): lax.all_to_all(block_scale[None], 'worker', split_axis=1, concat_axis=0,...]
    unnamed x4 -> x0, other arithmetic: 16 us -> none
    unnamed x10 -> x4, local copies, waits for them, and re-layouts: 20.2 us -> 5.54 us
  transfers between devices with their start and end apart: 3 -> 0, of which waited for: 2 -> 0; matrix products, arithmetic and copies ran while one was open for 12% -> 0% of each run, Pallas kernels for 0% -> 0%
where the time goes in v1:
time: 60.2 us
  Pallas kernels  54 us (90%)
  local copies, waits for them, and re-layouts  5.54 us (9%)
  between operations  0.65 us (1%)
    pallas_call x1, Pallas kernels, step(): pl.pallas_call(functools.partial(kernel, halves), out_shape=(jax.ShapeDty...  54 us
    unnamed x4, local copies, waits for them, and re-layouts  5.54 us

profile of v1, /device:TPU:1, one launch (start us, length us, event | category | flops | bytes accessed | tf_op | source)
XLA Modules:
  0.0 60.2 jit_solution(1129899702100411794)
XLA Ops:
  0.6 54.0 %shard_map.50 = (f32[256,4608]{1,0:T(8,128)}, f32[8,4608]{1,0:T(8,128)}) custom-call(bf16[1,256,4608]{2,1,0:T(8,128)(2,1)} %local_hbm.1, f32[256,4608]{1,0:T(8,128)} %base_hbm.1, f32[8,4608]{1,0:T(8,128)} %mom_hbm.1), custom_call_target="tpu_custom_call" | custom-call | tf_op jit(solution)/shard_map/pallas_call | solution.py:399
  54.6 0.0 copy-start
  54.6 4.9 %copy.7 = f32[256,4608]{1,0:T(8,128)} copy(f32[256,4608]{1,0:T(8,128)} %get-tuple-element.4) | data formatting | bytes 9437184
  59.5 0.0 copy-done
  59.5 0.7 %copy.8 = f32[8,4608]{1,0:T(8,128)} copy(f32[8,4608]{1,0:T(8,128)S(1)} %copy-done) | data formatting | bytes 294912
Async XLA Ops:
  54.6 4.9 %copy-start = (f32[8,4608]{1,0:T(8,128)S(1)}, f32[8,4608]{1,0:T(8,128)}, u32[]{:S(2)}) copy-start(f32[8,4608]{1,0:T(8,128)} %get-tuple-element.5) | copy-start | bytes 442372

commit v2 on v0

v2 whole, which is shorter than its diff:
```python
import functools
import math

import jax
import jax.numpy as jnp
from jax import lax
from jax.experimental import pallas as pl
from jax.experimental.pallas import tpu as pltpu
from jax.sharding import PartitionSpec as P

MESH = pl.DeviceIdType.MESH
F32 = jnp.float32
BF16 = jnp.bfloat16

BLOCK = 128
WORKERS = 32
EPSILON = 1e-06
CODE_LIMIT = 448.0
CLIP_WIDTH = 2.0
NESTEROV_MU = 0.9
OUTER_RATE = 0.7
ROOT = math.sqrt(BLOCK)

ZS, XS, CORES, PIECES = 4, 4, 2, 6
ROWS = 8
GROUP = 16
STRAIGHT_IN = (0, 1, 2, 3, 4, 5)
STRAIGHT_OUT = (0, 1, 2, 3, 4, 5)


def signs(size):
    row = lax.broadcasted_iota(jnp.int32, (size, size), 0)
    col = lax.broadcasted_iota(jnp.int32, (size, size), 1)
    common = jnp.bitwise_and(jnp.bitwise_and(row, col), BLOCK - 1)
    for shift in (4, 2, 1):
        common = jnp.bitwise_xor(common, jnp.right_shift(common, shift))
    sign = (1 - 2 * jnp.bitwise_and(common, 1)).astype(F32)
    same = jnp.right_shift(row, 7) == jnp.right_shift(col, 7)
    return jnp.where(same, sign, 0.0).astype(BF16), jnp.where(same, 1.0, 0.0).astype(BF16)


def limit_of(square_sum):
    mean = square_sum * (1.0 / BLOCK) + EPSILON
    scale = (mean * lax.rsqrt(mean) * (CLIP_WIDTH / CODE_LIMIT)).astype(BF16)
    return scale.astype(F32)


def rotate_exactly(values, table):
    high = values.astype(BF16)
    low = (values - high.astype(F32)).astype(BF16)
    return jnp.dot(high, table, preferred_element_type=F32) + jnp.dot(low, table, preferred_element_type=F32)


def kernel(
    tiles,
    local_hbm, base_hbm, mom_hbm,
    out_v, out_mom,
    local_v, base_v, mom_v, table2, ones2,
    enc, sib, ring_a, ring_c, ring_d, zsend, zrecv, acc, gath,
    in_sem, mom_sem,
    sib_s, sib_r, a_s, a_r, c_s, c_r, d_s, d_r, z_s, z_r,
    gz_s, gz_r, gf_s, gf_r, gh_s, gh_r, gp_s, gp_r,
):
    me = lax.axis_index("worker")
    z, x, core = me // 8, (me // 2) % 4, me % 2
    def at(z_, x_, core_):
        return {"worker": (z_ * XS + x_) * CORES + core_}

    xr, xl, xo = (x + 1) % XS, (x + XS - 1) % XS, (x + 2) % XS
    right, left, across, pair = at(z, xr, core), at(z, xl, core), at(z, xo, core), at(z, x, 1 - core)
    others = [(z + i) % ZS for i in range(1, ZS)]
    width = tiles * 2 * BLOCK

    def copy(src, dst, send, recv, device):
        return pltpu.make_async_remote_copy(
            src_ref=src, dst_ref=dst, send_sem=send, recv_sem=recv, device_id=device, device_id_type=MESH
        )

    sent = []

    def start(*args):
        one = copy(*args)
        one.start()
        sent.append(one)

    def arrived(spot, send, recv):
        copy(spot, spot, send, recv, pair).wait_recv()

    loads = []
    for k in range(PIECES):
        cols = pl.ds(k * width, width)
        loads.append((
            pltpu.make_async_copy(base_hbm.at[:, cols], base_v.at[:, cols], in_sem.at[k, 0]),
            pltpu.make_async_copy(local_hbm.at[0, :, cols], local_v.at[:, cols], in_sem.at[k, 1]),
        ))
        for one in loads[k]:
            one.start()
    mom_load = pltpu.make_async_copy(mom_hbm, mom_v, mom_sem)
    mom_load.start()

    barrier = pltpu.get_barrier_semaphore()
    greeted = [right, left, across, pair] + [at(zd, x, core) for zd in others]
    for device in greeted:
        pl.semaphore_signal(barrier, inc=1, device_id=device, device_id_type=MESH)

    table, ones = signs(2 * BLOCK)
    table2[...] = table
    ones2[...] = ones

    def enter():
        pl.semaphore_wait(barrier, len(greeted))

    def sides(k):
        return (xr, right, xl, left) if k % 2 == 0 else (xl, left, xr, right)

    def encode(k):
        for one in loads[k]:
            one.wait()
        for zd in range(ZS):
            rows = slice(zd * XS * GROUP, (zd + 1) * XS * GROUP)
            for t in range(tiles):
                cols = slice((k * tiles + t) * 256, (k * tiles + t + 1) * 256)
                diff = base_v[rows, cols] - local_v[rows, cols].astype(F32)
                turned = jnp.dot(diff.astype(BF16), table2[...], preferred_element_type=F32)
                square = jnp.dot((diff * diff).astype(BF16), ones2[...], preferred_element_type=F32)
                limit = limit_of(square) * (CODE_LIMIT * ROOT)
                value = jnp.minimum(jnp.maximum(turned, -limit), limit)
                for xd in range(XS):
                    for c in range(CORES):
                        r = xd * GROUP + c * ROWS
                        both = jnp.concatenate([value[r : r + ROWS, :BLOCK], value[r : r + ROWS, BLOCK:]], axis=0)
                        enc[c, k, xd, zd, :, t * BLOCK : (t + 1) * BLOCK] = both.astype(BF16)

    def send_pair(k):
        start(enc.at[1 - core, k], sib.at[k], sib_s.at[k], sib_r.at[k], pair)

    def add_pair(k):
        arrived(sib.at[k], sib_s.at[k], sib_r.at[k])
        xv, via, xw, other = sides(k)
        straight = k in STRAIGHT_IN
        for xd in (xo, xw, xv, x):
            enc[core, k, xd] = (enc[core, k, xd].astype(F32) + sib[k, xd].astype(F32)).astype(BF16)
            if xd is xo:
                start(enc.at[core, k, xo], ring_a.at[k], a_s.at[k], a_r.at[k], across if straight else via)
            elif xd is xw:
                start(enc.at[core, k, xw], ring_d.at[k], d_s.at[k], d_r.at[k], other)
            elif xd is xv and straight:
                start(enc.at[core, k, xv], ring_c.at[k], c_s.at[k], c_r.at[k], via)

    def add_far(k):
        xv, via, _, _ = sides(k)
        arrived(ring_a.at[k], a_s.at[k], a_r.at[k])
        enc[core, k, xv] = (enc[core, k, xv].astype(F32) + ring_a[k].astype(F32)).astype(BF16)
        start(enc.at[core, k, xv], ring_c.at[k], c_s.at[k], c_r.at[k], via)

    def add_ring(k):
        arrived(ring_d.at[k], d_s.at[k], d_r.at[k])
        arrived(ring_c.at[k], c_s.at[k], c_r.at[k])
        if k in STRAIGHT_IN:
            arrived(ring_a.at[k], a_s.at[k], a_r.at[k])

        def total(zd):
            here = enc[core, k, x, zd].astype(F32) + ring_c[k, zd].astype(F32) + ring_d[k, zd].astype(F32)
            return here + ring_a[k, zd].astype(F32) if k in STRAIGHT_IN else here

        for i, zd in enumerate(others):
            zsend[k, i] = total(zd).astype(BF16)
            start(zsend.at[k, i], zrecv.at[k, z], z_s.at[k, i], z_r.at[k, z], at(zd, x, core))
        acc[k] = total(z)

    def stacked(read):
        return jnp.concatenate([read(t) for t in range(tiles)], axis=0)

    def cut(array, t):
        return array[t * GROUP : (t + 1) * GROUP]

    def own(k):
        if k == 0:
            mom_load.wait()
        table1 = table2[:BLOCK, :BLOCK]
        summed = acc[k]
        for zs in others:
            arrived(zrecv.at[k, zs], z_s.at[k, 0], z_r.at[k, zs])
            summed = summed + zrecv[k, zs].astype(F32)
        total = stacked(lambda t: summed[:, t * BLOCK : (t + 1) * BLOCK])
        first = k * width
        momentum = stacked(
            lambda t: jnp.concatenate(
                [mom_v[:, first + b * BLOCK : first + (b + 1) * BLOCK] for b in (2 * t, 2 * t + 1)], axis=0
            )
        )
        pseudo = rotate_exactly(total, table1) * (1.0 / (BLOCK * WORKERS))
        new_momentum = NESTEROV_MU * momentum + pseudo
        outer_step = pseudo + NESTEROV_MU * new_momentum
        square = jnp.sum(outer_step * outer_step, axis=-1, keepdims=True)
        limit = limit_of(square) * CODE_LIMIT
        turned = rotate_exactly(outer_step, table1) * (1.0 / ROOT)
        value = jnp.minimum(jnp.maximum(turned, -limit), limit).astype(BF16)
        for t in range(tiles):
            gath[core, k, x, z, :, t * BLOCK : (t + 1) * BLOCK] = cut(value, t)
        spot = gath.at[core, k, x, z]
        for i, zd in enumerate(others):
            start(spot, spot, gz_s.at[k, i], gz_r.at[k, z], at(zd, x, core))
        for t in range(tiles):
            for b in range(2):
                cols = slice(first + (2 * t + b) * BLOCK, first + (2 * t + b + 1) * BLOCK)
                out_mom[:, cols] = cut(new_momentum, t)[b * ROWS : (b + 1) * ROWS]

    def to_pair(k, i, x_):
        spot = gath.at[core, k, x_]
        start(spot, spot, gp_s.at[k, i], gp_r.at[k, i], pair)

    def full(k):
        for zo in others:
            arrived(gath.at[core, k, x, zo], gz_s.at[k, 0], gz_r.at[k, zo])
        spot = gath.at[core, k, x]
        if k in STRAIGHT_OUT:
            start(spot, spot, gh_s.at[k], gh_r.at[k], across)
        start(spot, spot, gf_s.at[k, 0], gf_r.at[k, 0], right)
        start(spot, spot, gf_s.at[k, 1], gf_r.at[k, 1], left)
        to_pair(k, 0, x)

    def onward(k):
        ways = ((0, xl, right), (1, xr, left))
        for i, x_, device in ways if k % 2 == 0 else ways[::-1]:
            spot = gath.at[core, k, x_]
            arrived(spot, gf_s.at[k, i], gf_r.at[k, i])
            if i == k % 2 and k not in STRAIGHT_OUT:
                start(spot, spot, gh_s.at[k], gh_r.at[k], device)
            to_pair(k, 1 + i, x_)

    def far(k):
        arrived(gath.at[core, k, xo], gh_s.at[k], gh_r.at[k])
        to_pair(k, 3, xo)

    def decode(k, c, x_):
        table1 = table2[:BLOCK, :BLOCK]
        codes = jnp.concatenate(
            [stacked(lambda t: gath[c, k, x_, zo, :, t * BLOCK : (t + 1) * BLOCK]) for zo in range(ZS)], axis=0
        )
        back = jnp.dot(codes, table1, preferred_element_type=F32) * (OUTER_RATE / ROOT)
        for zo in range(ZS):
            rows = pl.ds(pl.multiple_of((zo * XS + x_) * GROUP + c * ROWS, ROWS), ROWS)
            for t in range(tiles):
                for b in range(2):
                    first = k * width + (2 * t + b) * BLOCK
                    cols = slice(first, first + BLOCK)
                    out_v[rows, cols] = base_v[rows, cols] - cut(back, zo * tiles + t)[b * ROWS : (b + 1) * ROWS]

    def finish(k):
        for x_ in (x, xl, xr, xo):
            decode(k, core, x_)
        for i, x_ in enumerate((x, xl, xr, xo)):
            arrived(gath.at[1 - core, k, x_], gp_s.at[k, i], gp_r.at[k, i])
            decode(k, 1 - core, x_)

    plan = (
        (encode, 0), (encode, 1), (encode, 2), (encode, 3), (encode, 4), (encode, 5), (enter,), (send_pair, 0),
        (send_pair, 1), (send_pair, 2), (send_pair, 3), (send_pair, 4), (send_pair, 5), (add_pair, 0), (add_pair, 1),
        (add_pair, 2), (add_pair, 3), (add_pair, 4), (add_pair, 5), (add_ring, 0), (add_ring, 1), (add_ring, 2),
        (own, 0), (add_ring, 3), (own, 1), (add_ring, 4), (own, 2), (full, 0), (add_ring, 5), (own, 3), (full, 1),
        (own, 4), (full, 2), (onward, 0), (far, 0), (own, 5), (finish, 0), (full, 3), (onward, 1), (far, 1), (full, 4),
        (finish, 1), (onward, 2), (far, 2), (full, 5), (finish, 2), (onward, 3), (far, 3), (finish, 3), (onward, 4),
        (far, 4), (finish, 4), (onward, 5), (far, 5), (finish, 5),
    )
    for act, *which in plan:
        act(*which)

    for one in sent:
        one.wait_send()


def step(local_w, base_w, momentum):
    rows, columns = base_w.shape
    tiles = columns // (256 * PIECES)
    dma = pltpu.SemaphoreType.DMA
    chunk = (GROUP, tiles * BLOCK)
    ring = (PIECES, ZS) + chunk
    held = (CORES, PIECES, XS, ZS) + chunk
    each = dma((PIECES,))
    return pl.pallas_call(
        functools.partial(kernel, tiles),
        out_shape=(pltpu.VMEM(base_w.shape, F32), pltpu.VMEM(momentum.shape, F32)),
        in_specs=[pl.BlockSpec(memory_space=pl.ANY)] * 3,
        out_specs=[pl.BlockSpec(memory_space=pltpu.VMEM)] * 2,
        scratch_shapes=[
            pltpu.VMEM((rows, columns), BF16),
            pltpu.VMEM((rows, columns), F32),
            pltpu.VMEM((ROWS, columns), F32),
            pltpu.VMEM((2 * BLOCK, 2 * BLOCK), BF16),
            pltpu.VMEM((2 * BLOCK, 2 * BLOCK), BF16),
            pltpu.VMEM(held, BF16),
            pltpu.VMEM((PIECES, XS, ZS) + chunk, BF16),
            pltpu.VMEM(ring, BF16),
            pltpu.VMEM(ring, BF16),
            pltpu.VMEM(ring, BF16),
            pltpu.VMEM((PIECES, ZS - 1) + chunk, BF16),
            pltpu.VMEM(ring, BF16),
            pltpu.VMEM((PIECES,) + chunk, F32),
            pltpu.VMEM(held, BF16),
            dma((PIECES, 2)), dma,
            each, each, each, each, each, each, each, each,
            dma((PIECES, ZS - 1)), dma((PIECES, ZS)),
            dma((PIECES, ZS - 1)), dma((PIECES, ZS)),
            dma((PIECES, 2)), dma((PIECES, 2)),
            each, each,
            dma((PIECES, 4)), dma((PIECES, 4)),
        ],
        compiler_params=pltpu.CompilerParams(
            collective_id=0, has_side_effects=True, vmem_limit_bytes=50 * 1024 * 1024
        ),
    )(*(pltpu.with_memory_space_constraint(a, pltpu.HBM) for a in (local_w, base_w, momentum)))


def solution(mesh):
    in_specs = (P("worker", "shard", None), P("shard", None), P(("shard", "worker"), None))
    out_specs = (P("shard", None), P(("shard", "worker"), None))
    return jax.shard_map(step, mesh=mesh, in_specs=in_specs, out_specs=out_specs, check_vma=False)
```

time: 241 us -> 47.4 us (0.20)
  waiting for transfers between devices: 72.4 us -> 0 us
  Pallas kernels: 0 us -> 43.8 us
  blocking collectives: 42.2 us -> 0 us
  local copies, waits for them, and re-layouts: 39.8 us -> 2.85 us
  other arithmetic: 33.5 us -> 0 us
  matrix products: 20.3 us -> 0 us
  starting transfers between devices: 18 us -> 0 us
  between operations: 14.2 us -> 0.64 us
    all_to_all x2 -> x0, waiting for transfers between devices: 53.1 us -> none  [the longest x1 53.1 us: shards(): lax.all_to_all(encoded[None], 'worker', split_axis=1, concat_axis=0, tile...]
    pallas_call x0 -> x1, Pallas kernels: none -> 43.8 us  [step(): pl.pallas_call(functools.partial(kernel, tiles), out_shape=(pltpu.VMEM(ba...]
    all_gather x1 -> x0, blocking collectives: 42.2 us -> none  [shards(): lax.all_gather(step_scale, 'worker', axis=0, tiled=True)]
    dot_general x4 -> x0, matrix products: 20.3 us -> none  [rotate(): turned = jnp.matmul(blocks, table, precision=lax.Precision.HIGHEST)]
    all_gather x1 -> x0, waiting for transfers between devices: 19.3 us -> none  [shards(): lax.all_gather(step_codes, 'worker', axis=0, tiled=True)]
    all_to_all x2 -> x0, starting transfers between devices: 17.8 us -> none  [the longest x1 10 us: shards(): lax.all_to_all(block_scale[None], 'worker', split_axis=1, concat_axis=0,...]
    unnamed x10 -> x2, local copies, waits for them, and re-layouts: 20.2 us -> 2.85 us
    unnamed x4 -> x0, other arithmetic: 16 us -> none
  transfers between devices with their start and end apart: 3 -> 0, of which waited for: 2 -> 0; matrix products, arithmetic and copies ran while one was open for 12% -> 0% of each run, Pallas kernels for 0% -> 0%
where the time goes in v2:
time: 47.4 us; the launch traced here: 47.3 us
  Pallas kernels  43.8 us (92%)
  local copies, waits for them, and re-layouts  2.85 us (6%)
  between operations  0.64 us (1%)
    pallas_call x1, Pallas kernels, step(): pl.pallas_call(functools.partial(kernel, tiles), out_shape=(pltpu.VMEM(ba...  43.8 us
    unnamed x2, local copies, waits for them, and re-layouts  2.85 us

profile of v2, /device:TPU:1, one launch (start us, length us, event | category | flops | bytes accessed | tf_op | source)
XLA Modules:
  0.0 47.3 jit_solution(1060966499397988466)
XLA Ops:
  0.6 43.8 %shard_map.50 = (f32[256,4608]{1,0:T(8,128)S(1)}, f32[8,4608]{1,0:T(8,128)S(1)}) custom-call(bf16[1,256,4608]{2,1,0:T(8,128)(2,1)} %local_hbm.1, f32[256,4608]{1,0:T(8,128)} %base_hbm.1, f32[8,4608]{1,0:T(8,128)} %mom_hbm.1), custom_call_target="tpu_custom_call" | custom-call | tf_op jit(solution)/shard_map/pallas_call | solution.py:281
  44.4 2.2 %copy.7 = f32[256,4608]{1,0:T(8,128)} copy(f32[256,4608]{1,0:T(8,128)S(1)} %get-tuple-element.2) | data formatting | bytes 9437184
  46.6 0.7 %copy.8 = f32[8,4608]{1,0:T(8,128)} copy(f32[8,4608]{1,0:T(8,128)S(1)} %get-tuple-element.3) | data formatting | bytes 294912

commit v3 on v2

--- a/solution.py
+++ b/solution.py
@@ -255,9 +255,9 @@
             decode(k, 1 - core, x_)
 
     plan = (
-        (encode, 0), (encode, 1), (encode, 2), (encode, 3), (encode, 4), (encode, 5), (enter,), (send_pair, 0),
-        (send_pair, 1), (send_pair, 2), (send_pair, 3), (send_pair, 4), (send_pair, 5), (add_pair, 0), (add_pair, 1),
-        (add_pair, 2), (add_pair, 3), (add_pair, 4), (add_pair, 5), (add_ring, 0), (add_ring, 1), (add_ring, 2),
+        (encode, 0), (enter,), (send_pair, 0), (encode, 1), (send_pair, 1), (encode, 2), (send_pair, 2), (encode, 3),
+        (send_pair, 3), (add_pair, 0), (add_pair, 1), (encode, 4), (send_pair, 4), (add_pair, 2), (encode, 5),
+        (send_pair, 5), (add_pair, 3), (add_pair, 4), (add_pair, 5), (add_ring, 0), (add_ring, 1), (add_ring, 2),
         (own, 0), (add_ring, 3), (own, 1), (add_ring, 4), (own, 2), (full, 0), (add_ring, 5), (own, 3), (full, 1),
         (own, 4), (full, 2), (onward, 0), (far, 0), (own, 5), (finish, 0), (full, 3), (onward, 1), (far, 1), (full, 4),
         (finish, 1), (onward, 2), (far, 2), (full, 5), (finish, 2), (onward, 3), (far, 3), (finish, 3), (onward, 4),
@@ -268,6 +268,22 @@
 
     for one in sent:
         one.wait_send()
+
+
+STORES = 8
+
+
+def store(base_v, mom_v, base_hbm, mom_hbm, sem):
+    rows = base_v.shape[0] // STORES
+    copies = [
+        pltpu.make_async_copy(base_v.at[pl.ds(i * rows, rows)], base_hbm.at[pl.ds(i * rows, rows)], sem.at[i])
+        for i in range(STORES)
+    ]
+    copies.append(pltpu.make_async_copy(mom_v, mom_hbm, sem.at[STORES]))
+    for one in copies:
+        one.start()
+    for one in copies:
+        one.wait()
 
 
 def step(local_w, base_w, momentum):
@@ -278,7 +294,7 @@
     ring = (PIECES, ZS) + chunk
     held = (CORES, PIECES, XS, ZS) + chunk
     each = dma((PIECES,))
-    return pl.pallas_call(
+    new_base, new_momentum = pl.pallas_call(
         functools.partial(kernel, tiles),
         out_shape=(pltpu.VMEM(base_w.shape, F32), pltpu.VMEM(momentum.shape, F32)),
         in_specs=[pl.BlockSpec(memory_space=pl.ANY)] * 3,
@@ -310,6 +326,14 @@
             collective_id=0, has_side_effects=True, vmem_limit_bytes=50 * 1024 * 1024
         ),
     )(*(pltpu.with_memory_space_constraint(a, pltpu.HBM) for a in (local_w, base_w, momentum)))
+    return pl.pallas_call(
+        store,
+        out_shape=(jax.ShapeDtypeStruct(base_w.shape, F32), jax.ShapeDtypeStruct(momentum.shape, F32)),
+        in_specs=[pl.BlockSpec(memory_space=pltpu.VMEM)] * 2,
+        out_specs=[pl.BlockSpec(memory_space=pl.ANY)] * 2,
+        scratch_shapes=[dma((STORES + 1,))],
+        compiler_params=pltpu.CompilerParams(vmem_limit_bytes=4 * 1024 * 1024),
+    )(*(pltpu.with_memory_space_constraint(a, pltpu.VMEM) for a in (new_base, new_momentum)))
 
 
 def solution(mesh):

time: 47.4 us -> 44.9 us (0.947)
  local copies, waits for them, and re-layouts: 2.85 us -> 0 us
    unnamed x2 -> x0, local copies, waits for them, and re-layouts: 2.85 us -> none
    pallas_call x0 -> x1, Pallas kernels: none -> 2.29 us  [step(): pl.pallas_call(store, out_shape=(jax.ShapeDtypeStruct(base_w.shape, F32),...]
    pallas_call x1, Pallas kernels: 43.8 us -> 41.8 us  [step(): pl.pallas_call(functools.partial(kernel, tiles), out_shape=(pltpu.VMEM(ba...]
where the time goes in v3:
time: 44.9 us; the launch traced here: 44.8 us
  Pallas kernels  44.1 us (98%)
  between operations  0.64 us (1%)
    pallas_call x1, Pallas kernels, step(): pl.pallas_call(functools.partial(kernel, tiles), out_shape=(pltpu.VMEM(ba...  41.8 us
    pallas_call x1, Pallas kernels, step(): pl.pallas_call(store, out_shape=(jax.ShapeDtypeStruct(base_w.shape, F32),...  2.29 us

profile of v3, /device:TPU:1, one launch (start us, length us, event | category | flops | bytes accessed | tf_op | source)
XLA Modules:
  0.0 44.8 jit_solution(12843987802578121317)
XLA Ops:
  0.6 41.8 %shard_map.50 = (f32[256,4608]{1,0:T(8,128)S(1)}, f32[8,4608]{1,0:T(8,128)S(1)}) custom-call(bf16[1,256,4608]{2,1,0:T(8,128)(2,1)} %local_hbm.1, f32[256,4608]{1,0:T(8,128)} %base_hbm.1, f32[8,4608]{1,0:T(8,128)} %mom_hbm.1), custom_call_target="tpu_custom_call" | custom-call | tf_op jit(solution)/shard_map/pallas_call | solution.py:297
  42.5 2.3 %shard_map.51 = (f32[256,4608]{1,0:T(8,128)}, f32[8,4608]{1,0:T(8,128)}) custom-call(f32[256,4608]{1,0:T(8,128)S(1)} %get-tuple-element.4.base_v, f32[8,4608]{1,0:T(8,128)S(1)} %get-tuple-element.5.mom_v), custom_call_target="tpu_custom_call" | custom-call | tf_op jit(solution)/shard_map/pallas_call | solution.py:329

commit v4 on v3

v4 whole, which is shorter than its diff:
```python
import functools
import math

import jax
import jax.numpy as jnp
from jax import lax
from jax.experimental import pallas as pl
from jax.experimental.pallas import tpu as pltpu
from jax.sharding import PartitionSpec as P

MESH = pl.DeviceIdType.MESH
F32 = jnp.float32
BF16 = jnp.bfloat16

BLOCK = 128
WORKERS = 32
EPSILON = 1e-06
CODE_LIMIT = 448.0
CLIP_WIDTH = 2.0
NESTEROV_MU = 0.9
OUTER_RATE = 0.7
ROOT = math.sqrt(BLOCK)

SIDE, CORES = 4, 2
ROWS = 8
GROUP = 16
STORES = 8
X, Z = 0, 1
PIECES = ((3, X, X), (3, Z, X), (3, X, X), (3, X, X), (3, X, Z), (3, X, X),)
COUNT = len(PIECES)


def signs(size):
    row = lax.broadcasted_iota(jnp.int32, (size, size), 0)
    col = lax.broadcasted_iota(jnp.int32, (size, size), 1)
    common = jnp.bitwise_and(jnp.bitwise_and(row, col), BLOCK - 1)
    for shift in (4, 2, 1):
        common = jnp.bitwise_xor(common, jnp.right_shift(common, shift))
    sign = (1 - 2 * jnp.bitwise_and(common, 1)).astype(F32)
    same = jnp.right_shift(row, 7) == jnp.right_shift(col, 7)
    return jnp.where(same, sign, 0.0).astype(BF16), jnp.where(same, 1.0, 0.0).astype(BF16)


def limit_of(square_sum):
    mean = square_sum * (1.0 / BLOCK) + EPSILON
    scale = (mean * lax.rsqrt(mean) * (CLIP_WIDTH / CODE_LIMIT)).astype(BF16)
    return scale.astype(F32)


def rotate_exactly(values, table):
    high = values.astype(BF16)
    low = (values - high.astype(F32)).astype(BF16)
    return jnp.dot(high, table, preferred_element_type=F32) + jnp.dot(low, table, preferred_element_type=F32)


def kernel(
    local_hbm, base_hbm, mom_hbm,
    out_v, out_mom,
    local_v, base_v, mom_v, table2, ones2,
    enc, sib, ring, part, parts, acc, gath,
    in_sem, mom_sem,
    sib_s, sib_r, ring_s, ring_r, part_s, part_r,
    near_s, near_r, own_s, own_r, rest_s, rest_r, pair_s, pair_r,
):
    me = lax.axis_index("worker")
    core = me % 2
    here = ((me // 2) % SIDE, me // 8)

    def at(x, z, c):
        return {"worker": (z * SIDE + x) * CORES + c}

    def peer(axis, off):
        there = list(here)
        there[axis] = (here[axis] + off) % SIDE
        return at(*there, core)

    pair = at(*here, 1 - core)
    offsets = (2, 1, 3)

    def copy(src, dst, send, recv, device):
        return pltpu.make_async_remote_copy(
            src_ref=src, dst_ref=dst, send_sem=send, recv_sem=recv, device_id=device, device_id_type=MESH
        )

    sent = []

    def start(*args):
        one = copy(*args)
        one.start()
        sent.append(one)

    def arrived(spot, send, recv):
        copy(spot, spot, send, recv, pair).wait_recv()

    firsts = [sum(size for size, _, _ in PIECES[:k]) for k in range(COUNT)]
    loads = []
    for k, (size, _, _) in enumerate(PIECES):
        cols = pl.ds(firsts[k] * 256, size * 256)
        loads.append((
            pltpu.make_async_copy(base_hbm.at[:, cols], base_v.at[:, cols], in_sem.at[k, 0]),
            pltpu.make_async_copy(local_hbm.at[0, :, cols], local_v.at[:, cols], in_sem.at[k, 1]),
        ))
        for one in loads[k]:
            one.start()
    mom_load = pltpu.make_async_copy(mom_hbm, mom_v, mom_sem)
    mom_load.start()

    barrier = pltpu.get_barrier_semaphore()
    greeted = [pair] + [peer(axis, off) for axis in (X, Z) for off in offsets]
    for device in greeted:
        pl.semaphore_signal(barrier, inc=1, device_id=device, device_id_type=MESH)

    table, ones = signs(2 * BLOCK)
    table2[...] = table
    ones2[...] = ones

    def enter():
        pl.semaphore_wait(barrier, len(greeted))

    def tile(t):
        return slice(t * BLOCK, (t + 1) * BLOCK)

    def stacked(size, read):
        return jnp.concatenate([read(t) for t in range(size)], axis=0)

    def cut(array, t):
        return array[t * GROUP : (t + 1) * GROUP]

    def encode(k):
        size, first_axis, _ = PIECES[k]
        for one in loads[k]:
            one.wait()
        for z in range(SIDE):
            rows = slice(z * SIDE * GROUP, (z + 1) * SIDE * GROUP)
            for t in range(size):
                cols = slice((firsts[k] + t) * 256, (firsts[k] + t + 1) * 256)
                diff = base_v[rows, cols] - local_v[rows, cols].astype(F32)
                turned = jnp.dot(diff.astype(BF16), table2[...], preferred_element_type=F32)
                square = jnp.dot((diff * diff).astype(BF16), ones2[...], preferred_element_type=F32)
                limit = limit_of(square) * (CODE_LIMIT * ROOT)
                value = jnp.minimum(jnp.maximum(turned, -limit), limit)
                for x in range(SIDE):
                    spot = (x, z) if first_axis == X else (z, x)
                    for c in range(CORES):
                        r = x * GROUP + c * ROWS
                        both = jnp.concatenate([value[r : r + ROWS, :BLOCK], value[r : r + ROWS, BLOCK:]], axis=0)
                        enc[k][c, *spot, :, tile(t)] = both.astype(BF16)

    def send_pair(k):
        start(enc[k].at[1 - core], sib[k], sib_s.at[k], sib_r.at[k], pair)

    def add_pair(k):
        axis = PIECES[k][1]
        arrived(sib[k], sib_s.at[k], sib_r.at[k])
        for off in offsets + (0,):
            to = (here[axis] + off) % SIDE
            enc[k][core, to] = (enc[k][core, to].astype(F32) + sib[k][to].astype(F32)).astype(BF16)
            if off:
                start(
                    enc[k].at[core, to], ring[k].at[off - 1], ring_s.at[k, off - 1], ring_r.at[k, off - 1],
                    peer(axis, off),
                )

    def add_first(k):
        axis = PIECES[k][1]
        for off in offsets:
            arrived(ring[k].at[off - 1], ring_s.at[k, off - 1], ring_r.at[k, off - 1])

        def total(to):
            there = enc[k][core, here[axis], to].astype(F32)
            for off in offsets:
                there = there + ring[k][off - 1, to].astype(F32)
            return there

        for off in offsets:
            part[k][off - 1] = total((here[1 - axis] + off) % SIDE).astype(BF16)
            start(
                part[k].at[off - 1], parts[k].at[off - 1], part_s.at[k, off - 1], part_r.at[k, off - 1],
                peer(1 - axis, off),
            )
        acc[k][...] = total(here[1 - axis])

    def own(k):
        if k == 0:
            mom_load.wait()
        size, _, axis = PIECES[k]
        table1 = table2[:BLOCK, :BLOCK]
        summed = acc[k][...]
        for off in offsets:
            arrived(parts[k].at[off - 1], part_s.at[k, off - 1], part_r.at[k, off - 1])
            summed = summed + parts[k][off - 1].astype(F32)
        total = stacked(size, lambda t: summed[:, tile(t)])
        blocks = [2 * (firsts[k] + t) for t in range(size)]
        momentum = stacked(
            size, lambda t: jnp.concatenate([mom_v[:, tile(blocks[t])], mom_v[:, tile(blocks[t] + 1)]], axis=0)
        )
        pseudo = rotate_exactly(total, table1) * (1.0 / (BLOCK * WORKERS))
        new_momentum = NESTEROV_MU * momentum + pseudo
        outer_step = pseudo + NESTEROV_MU * new_momentum
        square = jnp.sum(outer_step * outer_step, axis=-1, keepdims=True)
        limit = limit_of(square) * CODE_LIMIT
        turned = rotate_exactly(outer_step, table1) * (1.0 / ROOT)
        value = jnp.minimum(jnp.maximum(turned, -limit), limit).astype(BF16)
        for t in range(size):
            gath[k][core, here[axis], 0, :, tile(t)] = cut(value, t)
        spot = gath[k].at[core, here[axis], 0]
        for off in offsets:
            start(
                spot, gath[k].at[core, here[axis], SIDE - off], near_s.at[k, off - 1], near_r.at[k, off - 1],
                peer(1 - axis, off),
            )
        for off in offsets:
            start(spot, spot, own_s.at[k, off - 1], own_r.at[k, off - 1], peer(axis, off))
        for t in range(size):
            for b in range(2):
                out_mom[:, tile(blocks[t] + b)] = cut(new_momentum, t)[b * ROWS : (b + 1) * ROWS]

    def to_pair(k, i, place):
        spot = gath[k].at[core, place]
        start(spot, spot, pair_s.at[k, i], pair_r.at[k, i], pair)

    def spread(k):
        axis = PIECES[k][2]
        place = here[axis]
        for off in offsets:
            arrived(gath[k].at[core, place, SIDE - off], near_s.at[k, off - 1], near_r.at[k, off - 1])
        spot = gath[k].at[core, place, pl.ds(1, SIDE - 1)]
        for off in offsets:
            start(spot, spot, rest_s.at[k, off - 1], rest_r.at[k, off - 1], peer(axis, off))
        to_pair(k, 0, place)

    def collect(k):
        axis = PIECES[k][2]
        for off in (1, 3, 2):
            place = (here[axis] + SIDE - off) % SIDE
            arrived(gath[k].at[core, place, 0], own_s.at[k, off - 1], own_r.at[k, off - 1])
            arrived(gath[k].at[core, place, pl.ds(1, SIDE - 1)], rest_s.at[k, off - 1], rest_r.at[k, off - 1])
            to_pair(k, off, place)

    def decode(k, c, place):
        size, _, axis = PIECES[k]
        table1 = table2[:BLOCK, :BLOCK]
        codes = jnp.concatenate(
            [stacked(size, lambda t: gath[k][c, place, n, :, tile(t)]) for n in range(SIDE)], axis=0
        )
        back = jnp.dot(codes, table1, preferred_element_type=F32) * (OUTER_RATE / ROOT)
        for n in range(SIDE):
            near = (here[1 - axis] + n) % SIDE
            x, z = (place, near) if axis == X else (near, place)
            rows = pl.ds(pl.multiple_of((z * SIDE + x) * GROUP + c * ROWS, ROWS), ROWS)
            for t in range(size):
                for b in range(2):
                    cols = tile(2 * (firsts[k] + t) + b)
                    out_v[rows, cols] = base_v[rows, cols] - cut(back, n * size + t)[b * ROWS : (b + 1) * ROWS]

    def finish(k):
        axis = PIECES[k][2]
        places = [(here[axis] + SIDE - off) % SIDE for off in range(SIDE)]
        for off in (0, 1, 3, 2):
            decode(k, core, places[off])
        for off in (0, 1, 3, 2):
            arrived(gath[k].at[1 - core, places[off]], pair_s.at[k, off], pair_r.at[k, off])
            decode(k, 1 - core, places[off])

    plan = (
        (encode, 0), (enter,), (send_pair, 0), (encode, 1), (send_pair, 1), (encode, 2), (send_pair, 2), (encode, 3),
        (send_pair, 3), (add_pair, 0), (add_pair, 1), (encode, 4), (send_pair, 4), (add_pair, 2), (add_pair, 3),
        (encode, 5), (send_pair, 5), (add_pair, 4), (add_pair, 5), (add_first, 0), (add_first, 2), (add_first, 1),
        (add_first, 3), (own, 0), (add_first, 4), (own, 2), (add_first, 5), (own, 3), (own, 1), (spread, 0), (own, 4),
        (spread, 2), (own, 5), (collect, 0), (spread, 3), (spread, 4), (spread, 1), (finish, 0), (collect, 2),
        (finish, 2), (spread, 5), (collect, 3), (finish, 3), (collect, 1), (finish, 1), (collect, 4), (collect, 5),
        (finish, 4), (finish, 5),
    )
    for act, *which in plan:
        act(*which)

    for one in sent:
        one.wait_send()


def store(base_v, mom_v, base_hbm, mom_hbm, sem):
    rows = base_v.shape[0] // STORES
    copies = [
        pltpu.make_async_copy(base_v.at[pl.ds(i * rows, rows)], base_hbm.at[pl.ds(i * rows, rows)], sem.at[i])
        for i in range(STORES)
    ]
    copies.append(pltpu.make_async_copy(mom_v, mom_hbm, sem.at[STORES]))
    for one in copies:
        one.start()
    for one in copies:
        one.wait()


def step(local_w, base_w, momentum):
    rows, columns = base_w.shape
    dma = pltpu.SemaphoreType.DMA
    three = dma((COUNT, SIDE - 1))

    def each(*dims, dtype=BF16):
        return [pltpu.VMEM(dims + (GROUP, size * BLOCK), dtype) for size, _, _ in PIECES]

    new_base, new_momentum = pl.pallas_call(
        kernel,
        out_shape=(pltpu.VMEM(base_w.shape, F32), pltpu.VMEM(momentum.shape, F32)),
        in_specs=[pl.BlockSpec(memory_space=pl.ANY)] * 3,
        out_specs=[pl.BlockSpec(memory_space=pltpu.VMEM)] * 2,
        scratch_shapes=[
            pltpu.VMEM((rows, columns), BF16),
            pltpu.VMEM((rows, columns), F32),
            pltpu.VMEM((ROWS, columns), F32),
            pltpu.VMEM((2 * BLOCK, 2 * BLOCK), BF16),
            pltpu.VMEM((2 * BLOCK, 2 * BLOCK), BF16),
            each(CORES, SIDE, SIDE),
            each(SIDE, SIDE),
            each(SIDE - 1, SIDE),
            each(SIDE - 1),
            each(SIDE - 1),
            each(dtype=F32),
            each(CORES, SIDE, SIDE),
            dma((COUNT, 2)), dma,
            dma((COUNT,)), dma((COUNT,)), three, three, three, three,
            three, three, three, three, three, three, dma((COUNT, SIDE)), dma((COUNT, SIDE)),
        ],
        compiler_params=pltpu.CompilerParams(
            collective_id=0, has_side_effects=True, vmem_limit_bytes=50 * 1024 * 1024
        ),
    )(*(pltpu.with_memory_space_constraint(a, pltpu.HBM) for a in (local_w, base_w, momentum)))
    return pl.pallas_call(
        store,
        out_shape=(jax.ShapeDtypeStruct(base_w.shape, F32), jax.ShapeDtypeStruct(momentum.shape, F32)),
        in_specs=[pl.BlockSpec(memory_space=pltpu.VMEM)] * 2,
        out_specs=[pl.BlockSpec(memory_space=pl.ANY)] * 2,
        scratch_shapes=[dma((STORES + 1,))],
        compiler_params=pltpu.CompilerParams(vmem_limit_bytes=4 * 1024 * 1024),
    )(*(pltpu.with_memory_space_constraint(a, pltpu.VMEM) for a in (new_base, new_momentum)))


def solution(mesh):
    in_specs = (P("worker", "shard", None), P("shard", None), P(("shard", "worker"), None))
    out_specs = (P("shard", None), P(("shard", "worker"), None))
    return jax.shard_map(step, mesh=mesh, in_specs=in_specs, out_specs=out_specs, check_vma=False)
```

time: 44.9 us -> 43.6 us (0.971)
  Pallas kernels: 44.1 us -> 42.9 us
    pallas_call x1, Pallas kernels: 41.8 us -> 40.6 us  [step(): pl.pallas_call(kernel, out_shape=(pltpu.VMEM(base_w.shape, F32), pltpu.VM...]
where the time goes in v4:
time: 43.6 us; the launch traced here: 43.5 us
  Pallas kernels  42.9 us (98%)
  between operations  0.64 us (1%)
    pallas_call x1, Pallas kernels, step(): pl.pallas_call(kernel, out_shape=(pltpu.VMEM(base_w.shape, F32), pltpu.VM...  40.6 us
    pallas_call x1, Pallas kernels, step(): pl.pallas_call(store, out_shape=(jax.ShapeDtypeStruct(base_w.shape, F32),...  2.29 us

profile of v4, /device:TPU:1, one launch (start us, length us, event | category | flops | bytes accessed | tf_op | source)
XLA Modules:
  0.0 43.5 jit_solution(12426489079618790160)
XLA Ops:
  0.6 40.6 %shard_map.50 = (f32[256,4608]{1,0:T(8,128)S(1)}, f32[8,4608]{1,0:T(8,128)S(1)}) custom-call(bf16[1,256,4608]{2,1,0:T(8,128)(2,1)} %local_hbm.1, f32[256,4608]{1,0:T(8,128)} %base_hbm.1, f32[8,4608]{1,0:T(8,128)} %mom_hbm.1), custom_call_target="tpu_custom_call" | custom-call | tf_op jit(solution)/shard_map/pallas_call | solution.py:302
  41.2 2.3 %shard_map.51 = (f32[256,4608]{1,0:T(8,128)}, f32[8,4608]{1,0:T(8,128)}) custom-call(f32[256,4608]{1,0:T(8,128)S(1)} %get-tuple-element.4.base_v, f32[8,4608]{1,0:T(8,128)S(1)} %get-tuple-element.5.mom_v), custom_call_target="tpu_custom_call" | custom-call | tf_op jit(solution)/shard_map/pallas_call | solution.py:328

commit v5 on v4

--- a/solution.py
+++ b/solution.py
@@ -26,8 +26,9 @@
 GROUP = 16
 STORES = 8
 X, Z = 0, 1
-PIECES = ((3, X, X), (3, Z, X), (3, X, X), (3, X, X), (3, X, Z), (3, X, X),)
+PIECES = ((2, X, X), (2, Z, X), (2, X, X), (2, X, X), (2, X, X), (2, X, X), (2, X, Z), (2, X, X), (2, X, X),)
 COUNT = len(PIECES)
+EARLY = (0, 1, 2, 3)
 
 
 def signs(size):
@@ -60,7 +61,7 @@
     enc, sib, ring, part, parts, acc, gath,
     in_sem, mom_sem,
     sib_s, sib_r, ring_s, ring_r, part_s, part_r,
-    near_s, near_r, own_s, own_r, rest_s, rest_r, pair_s, pair_r,
+    near_s, near_r, far_s, far_r, pair_s, pair_r,
 ):
     me = lax.axis_index("worker")
     core = me % 2
@@ -82,15 +83,14 @@
             src_ref=src, dst_ref=dst, send_sem=send, recv_sem=recv, device_id=device, device_id_type=MESH
         )
 
-    sent = []
-
     def start(*args):
-        one = copy(*args)
-        one.start()
-        sent.append(one)
-
-    def arrived(spot, send, recv):
-        copy(spot, spot, send, recv, pair).wait_recv()
+        copy(*args).start()
+
+    def arrived(spot, recv):
+        copy(spot, spot, in_sem.at[0, 0], recv, pair).wait_recv()
+
+    def left(spot, send):
+        copy(spot, spot, send, in_sem.at[0, 0], pair).wait_send()
 
     firsts = [sum(size for size, _, _ in PIECES[:k]) for k in range(COUNT)]
     loads = []
@@ -151,20 +151,16 @@
 
     def add_pair(k):
         axis = PIECES[k][1]
-        arrived(sib[k], sib_s.at[k], sib_r.at[k])
+        arrived(sib[k], sib_r.at[k])
         for off in offsets + (0,):
             to = (here[axis] + off) % SIDE
             enc[k][core, to] = (enc[k][core, to].astype(F32) + sib[k][to].astype(F32)).astype(BF16)
             if off:
-                start(
-                    enc[k].at[core, to], ring[k].at[off - 1], ring_s.at[k, off - 1], ring_r.at[k, off - 1],
-                    peer(axis, off),
-                )
+                start(enc[k].at[core, to], ring[k].at[off - 1], ring_s.at[k], ring_r.at[k], peer(axis, off))
 
     def add_first(k):
         axis = PIECES[k][1]
-        for off in offsets:
-            arrived(ring[k].at[off - 1], ring_s.at[k, off - 1], ring_r.at[k, off - 1])
+        arrived(ring[k], ring_r.at[k])
 
         def total(to):
             there = enc[k][core, here[axis], to].astype(F32)
@@ -174,10 +170,7 @@
 
         for off in offsets:
             part[k][off - 1] = total((here[1 - axis] + off) % SIDE).astype(BF16)
-            start(
-                part[k].at[off - 1], parts[k].at[off - 1], part_s.at[k, off - 1], part_r.at[k, off - 1],
-                peer(1 - axis, off),
-            )
+            start(part[k].at[off - 1], parts[k].at[off - 1], part_s.at[k], part_r.at[k], peer(1 - axis, off))
         acc[k][...] = total(here[1 - axis])
 
     def own(k):
@@ -186,8 +179,8 @@
         size, _, axis = PIECES[k]
         table1 = table2[:BLOCK, :BLOCK]
         summed = acc[k][...]
+        arrived(parts[k], part_r.at[k])
         for off in offsets:
-            arrived(parts[k].at[off - 1], part_s.at[k, off - 1], part_r.at[k, off - 1])
             summed = summed + parts[k][off - 1].astype(F32)
         total = stacked(size, lambda t: summed[:, tile(t)])
         blocks = [2 * (firsts[k] + t) for t in range(size)]
@@ -205,37 +198,38 @@
             gath[k][core, here[axis], 0, :, tile(t)] = cut(value, t)
         spot = gath[k].at[core, here[axis], 0]
         for off in offsets:
-            start(
-                spot, gath[k].at[core, here[axis], SIDE - off], near_s.at[k, off - 1], near_r.at[k, off - 1],
-                peer(1 - axis, off),
-            )
-        for off in offsets:
-            start(spot, spot, own_s.at[k, off - 1], own_r.at[k, off - 1], peer(axis, off))
+            start(spot, gath[k].at[core, here[axis], SIDE - off], near_s.at[k], near_r.at[k], peer(1 - axis, off))
+        if k in EARLY:
+            for off in offsets:
+                start(spot, spot, far_s.at[k], far_r.at[k, off - 1], peer(axis, off))
         for t in range(size):
             for b in range(2):
                 out_mom[:, tile(blocks[t] + b)] = cut(new_momentum, t)[b * ROWS : (b + 1) * ROWS]
 
-    def to_pair(k, i, place):
+    def to_pair(k, place):
         spot = gath[k].at[core, place]
-        start(spot, spot, pair_s.at[k, i], pair_r.at[k, i], pair)
+        start(spot, spot, pair_s.at[k], pair_r.at[k], pair)
 
     def spread(k):
         axis = PIECES[k][2]
         place = here[axis]
+        spot = gath[k].at[core, place, pl.ds(1, SIDE - 1)]
+        arrived(spot, near_r.at[k])
+        if k not in EARLY:
+            spot = gath[k].at[core, place]
         for off in offsets:
-            arrived(gath[k].at[core, place, SIDE - off], near_s.at[k, off - 1], near_r.at[k, off - 1])
-        spot = gath[k].at[core, place, pl.ds(1, SIDE - 1)]
-        for off in offsets:
-            start(spot, spot, rest_s.at[k, off - 1], rest_r.at[k, off - 1], peer(axis, off))
-        to_pair(k, 0, place)
+            start(spot, spot, far_s.at[k], far_r.at[k, off - 1], peer(axis, off))
+        to_pair(k, place)
+        left(sib[k], sib_s.at[k])
+        left(ring[k], ring_s.at[k])
+        left(part[k], part_s.at[k])
 
     def collect(k):
         axis = PIECES[k][2]
         for off in (1, 3, 2):
             place = (here[axis] + SIDE - off) % SIDE
-            arrived(gath[k].at[core, place, 0], own_s.at[k, off - 1], own_r.at[k, off - 1])
-            arrived(gath[k].at[core, place, pl.ds(1, SIDE - 1)], rest_s.at[k, off - 1], rest_r.at[k, off - 1])
-            to_pair(k, off, place)
+            arrived(gath[k].at[core, place], far_r.at[k, off - 1])
+            to_pair(k, place)
 
     def decode(k, c, place):
         size, _, axis = PIECES[k]
@@ -258,24 +252,27 @@
         places = [(here[axis] + SIDE - off) % SIDE for off in range(SIDE)]
         for off in (0, 1, 3, 2):
             decode(k, core, places[off])
+        arrived(gath[k].at[1 - core], pair_r.at[k])
         for off in (0, 1, 3, 2):
-            arrived(gath[k].at[1 - core, places[off]], pair_s.at[k, off], pair_r.at[k, off])
             decode(k, 1 - core, places[off])
+        left(part[k], near_s.at[k])
+        left(ring[k], far_s.at[k])
+        left(gath[k].at[core], pair_s.at[k])
 
     plan = (
-        (encode, 0), (enter,), (send_pair, 0), (encode, 1), (send_pair, 1), (encode, 2), (send_pair, 2), (encode, 3),
-        (send_pair, 3), (add_pair, 0), (add_pair, 1), (encode, 4), (send_pair, 4), (add_pair, 2), (add_pair, 3),
-        (encode, 5), (send_pair, 5), (add_pair, 4), (add_pair, 5), (add_first, 0), (add_first, 2), (add_first, 1),
-        (add_first, 3), (own, 0), (add_first, 4), (own, 2), (add_first, 5), (own, 3), (own, 1), (spread, 0), (own, 4),
-        (spread, 2), (own, 5), (collect, 0), (spread, 3), (spread, 4), (spread, 1), (finish, 0), (collect, 2),
-        (finish, 2), (spread, 5), (collect, 3), (finish, 3), (collect, 1), (finish, 1), (collect, 4), (collect, 5),
-        (finish, 4), (finish, 5),
+        (encode, 0), (encode, 1), (enter,), (send_pair, 0), (send_pair, 1), (encode, 2), (send_pair, 2), (encode, 3),
+        (send_pair, 3), (encode, 4), (send_pair, 4), (add_pair, 0), (add_pair, 1), (add_pair, 2), (encode, 5),
+        (send_pair, 5), (add_pair, 3), (add_pair, 4), (encode, 6), (send_pair, 6), (encode, 7), (send_pair, 7),
+        (add_pair, 5), (encode, 8), (send_pair, 8), (add_pair, 6), (add_pair, 7), (add_pair, 8), (add_first, 0),
+        (add_first, 2), (add_first, 1), (add_first, 3), (own, 0), (add_first, 4), (own, 2), (add_first, 5), (own, 3),
+        (add_first, 6), (spread, 0), (add_first, 7), (own, 4), (spread, 2), (add_first, 8), (own, 5), (own, 1),
+        (spread, 3), (own, 6), (collect, 0), (own, 7), (spread, 4), (finish, 0), (collect, 2), (own, 8), (spread, 5),
+        (finish, 2), (spread, 1), (collect, 3), (spread, 6), (spread, 7), (finish, 3), (collect, 4), (spread, 8),
+        (finish, 4), (collect, 5), (collect, 1), (finish, 5), (collect, 7), (finish, 1), (collect, 6), (collect, 8),
+        (finish, 7), (finish, 6), (finish, 8),
     )
     for act, *which in plan:
         act(*which)
-
-    for one in sent:
-        one.wait_send()
 
 
 def store(base_v, mom_v, base_hbm, mom_hbm, sem):
@@ -294,7 +291,7 @@
 def step(local_w, base_w, momentum):
     rows, columns = base_w.shape
     dma = pltpu.SemaphoreType.DMA
-    three = dma((COUNT, SIDE - 1))
+    one = dma((COUNT,))
 
     def each(*dims, dtype=BF16):
         return [pltpu.VMEM(dims + (GROUP, size * BLOCK), dtype) for size, _, _ in PIECES]
@@ -318,8 +315,8 @@
             each(dtype=F32),
             each(CORES, SIDE, SIDE),
             dma((COUNT, 2)), dma,
-            dma((COUNT,)), dma((COUNT,)), three, three, three, three,
-            three, three, three, three, three, three, dma((COUNT, SIDE)), dma((COUNT, SIDE)),
+            one, one, one, one, one, one,
+            one, one, one, dma((COUNT, SIDE - 1)), one, one,
         ],
         compiler_params=pltpu.CompilerParams(
             collective_id=0, has_side_effects=True, vmem_limit_bytes=50 * 1024 * 1024

time: 43.6 us -> 40.6 us (0.931)
  Pallas kernels: 42.9 us -> 39.9 us
    pallas_call x1, Pallas kernels: 40.6 us -> 37.6 us  [step(): pl.pallas_call(kernel, out_shape=(pltpu.VMEM(base_w.shape, F32), pltpu.VM...]
where the time goes in v5:
time: 40.6 us
  Pallas kernels  39.9 us (98%)
  between operations  0.64 us (2%)
    pallas_call x1, Pallas kernels, step(): pl.pallas_call(kernel, out_shape=(pltpu.VMEM(base_w.shape, F32), pltpu.VM...  37.6 us
    pallas_call x1, Pallas kernels, step(): pl.pallas_call(store, out_shape=(jax.ShapeDtypeStruct(base_w.shape, F32),...  2.29 us

profile of v5, /device:TPU:1, one launch (start us, length us, event | category | flops | bytes accessed | tf_op | source)
XLA Modules:
  0.0 40.6 jit_solution(7890915344394788178)
XLA Ops:
  0.6 37.6 %shard_map.50 = (f32[256,4608]{1,0:T(8,128)S(1)}, f32[8,4608]{1,0:T(8,128)S(1)}) custom-call(bf16[1,256,4608]{2,1,0:T(8,128)(2,1)} %local_hbm.1, f32[256,4608]{1,0:T(8,128)} %base_hbm.1, f32[8,4608]{1,0:T(8,128)} %mom_hbm.1), custom_call_target="tpu_custom_call" | custom-call | tf_op jit(solution)/shard_map/pallas_call | solution.py:299
  38.3 2.3 %shard_map.51 = (f32[256,4608]{1,0:T(8,128)}, f32[8,4608]{1,0:T(8,128)}) custom-call(f32[256,4608]{1,0:T(8,128)S(1)} %get-tuple-element.4.base_v, f32[8,4608]{1,0:T(8,128)S(1)} %get-tuple-element.5.mom_v), custom_call_target="tpu_custom_call" | custom-call | tf_op jit(solution)/shard_map/pallas_call | solution.py:325
